TPU v7x, 256 devices: a whole 4x4x8 slice. The times are simulated.
256 devices in a mesh: pos: 64 (over x, z, core), pix: 4 (over y).
Axes of the slice: x: 4, y: 4, z: 8, core: 2. Of those that a mesh axis runs over, the one named last changes fastest.
Arguments:
- data: bfloat16 [65536, 16384], P('pos', 'pix'), may hold values from -64 to 64
- sketch_matrix: bfloat16 [16384, 256], P('pix'), may hold values from -0.046875 to 0.046875
Outputs:
- basis: float32 [65536, 256], P('pos')
- factor: float32 [256, 256], replicated
All inputs are finite; a program needn't handle non-finite values.
Results may differ from a plain program's by a relative error of at most 0.0028.
Values may be sent and summed in bfloat16 or wider, within the bound.
A program may use at most 128 MiB of HBM per device.

v0:
```python
import jax
import jax.numpy as jnp
from jax import lax
from jax.sharding import PartitionSpec as P


def pixel_total(partial_value):
    return lax.psum(partial_value, "pix")


def gram_of(sketch):
    return jnp.dot(
        sketch.T, sketch, precision=lax.Precision.HIGHEST, preferred_element_type=jnp.float32
    )


def orthonormal(sketch, total):
    gram = lax.psum(gram_of(sketch), "pos") / total
    lower = jnp.linalg.cholesky(gram)
    basis = jax.scipy.linalg.solve_triangular(lower, sketch.T, lower=True).T
    return (basis, lower)


def per_device(data, sketch_matrix):
    rows = data.shape[0]
    total = rows * lax.axis_size("pos")
    first = pixel_total(jnp.dot(data, sketch_matrix, preferred_element_type=jnp.float32))
    ortho, lower_one = orthonormal(first, total)
    ortho = ortho.astype(jnp.bfloat16)
    loading_term = lax.dot_general(
        data, ortho, (((0,), (0,)), ((), ())), preferred_element_type=jnp.float32
    )
    summed = lax.psum(loading_term, "pos")
    loads = (summed / total).astype(jnp.bfloat16)
    partial_value = jnp.dot(data, loads, preferred_element_type=jnp.float32)
    second = pixel_total(partial_value)
    basis, lower_two = orthonormal(second, total)
    return (basis, lower_two.T)


def solution(mesh):
    in_specs = (P("pos", "pix"), P("pix", None))
    out_specs = (P("pos", None), P())
    return jax.shard_map(
        per_device, mesh=mesh, in_specs=in_specs, out_specs=out_specs, check_vma=False
    )
```

profile of v0, /device:TPU:1, one launch (start us, length us, event | category | flops | bytes accessed | tf_op | source)
XLA Modules:
  0.0 842.9 jit_solution(979778920496642384)
XLA Ops:
  7.2 1.5 copy-done
  8.8 6.7 fusion.30
  15.5 53.5 %all-reduce.7.cloned.1.call-done = f32[1024,256]{1,0:T(8,128)} async-done(((f32[1024,256]{1,0:T(8,128)}), f32[1024,256]{1,0:T(8,128)}) %all-reduce.7.cloned.1.call-update) | async-done | bytes 1048592 | tf_op jit(solution)/shard_map/psum | solution.py:8
  69.0 4.1 fusion.31
  73.5 177.7 %all-reduce.9.cloned.1.call-done = f32[256,256]{0,1:T(8,128)} async-done(((f32[256,256]{0,1:T(8,128)}), f32[256,256]{0,1:T(8,128)}) %all-reduce.9.cloned.1.call-update) | async-done | bytes 262160 | tf_op jit(solution)/shard_map/psum | solution.py:18
  251.2 1.7 broadcast_multiply_fusion.1
  252.9 1.1 copy.5
  254.0 1.0 fusion.8
  255.0 0.7 copy-done.6
  255.7 11.7 %cholesky.130 = f32[128,128]{1,0:T(8,128)S(1)} custom-call(f32[128,128]{1,0:T(8,128)S(1)} %cholesky.194), custom_call_target="Cholesky" | custom-call | tf_op jit(solution)/shard_map/jit(cholesky)/cholesky | solution.py:19
  267.4 9.8 %custom-call.13 = f32[1,128,128]{1,2,0:T(8,128)S(1)} custom-call(f32[1,128,128]{2,1,0:T(8,128)S(1)} %get-tuple-element.51), custom_call_target="InvertDiagBlocksLowerTriangular" | custom-call | tf_op jit(solution)/shard_map/jit(cholesky)/cholesky | solution.py:19
  277.3 1.0 constant_dynamic-update-slice_fusion.3
  278.3 1.1 convolution_subtract_fusion.3
  279.4 11.7 %cholesky.147 = f32[128,128]{1,0:T(8,128)S(1)} custom-call(f32[128,128]{1,0:T(8,128)S(1)} %convolution_subtract_fusion.3), custom_call_target="Cholesky" | custom-call | tf_op jit(solution)/shard_map/jit(cholesky)/cholesky | solution.py:19
  291.2 0.7 compare_reduce_fusion.2
  293.2 1.0 select_select_fusion
  294.2 4.6 while.4
  295.4 1.4 bitcast_dynamic-update-slice_fusion.4
  297.4 1.4 bitcast_dynamic-update-slice_fusion.4
  298.9 20.3 %custom-call.14 = f32[2,128,128]{1,2,0:T(8,128)} custom-call(f32[2,128,128]{2,1,0:T(8,128)S(1)} %get-tuple-element.18), custom_call_target="InvertDiagBlocksLowerTriangular" | custom-call | tf_op jit(solution)/shard_map/jit(_solve_triangular)/triangular_solve | solution.py:20
  319.2 1.5 fusion.5
  320.7 1.0 convolution_subtract_fusion.1
  321.7 1.5 fusion.17
  323.2 7.7 convolution_bitcast_fusion
  331.0 191.6 %all-reduce.11.cloned.1.call-done = f32[4096,256]{0,1:T(8,128)} async-done(((f32[4096,256]{0,1:T(8,128)}), f32[4096,256]{0,1:T(8,128)}) %all-reduce.11.cloned.1.call-update) | async-done | bytes 4194320 | tf_op jit(solution)/shard_map/psum | solution.py:33
  522.6 8.0 fusion.2
  530.8 49.7 %all-reduce.13.cloned.1.call-done = f32[1024,256]{0,1:T(8,128)} async-done(((f32[1024,256]{0,1:T(8,128)}), f32[1024,256]{0,1:T(8,128)}) %all-reduce.13.cloned.1.call-update) | async-done | bytes 1048592 | tf_op jit(solution)/shard_map/psum | solution.py:8
  580.5 3.4 fusion.32
  583.9 178.3 %all-reduce.15.cloned.1.call-done = f32[256,256]{0,1:T(8,128)} async-done(((f32[256,256]{0,1:T(8,128)}), f32[256,256]{0,1:T(8,128)}) %all-reduce.15.cloned.1.call-update) | async-done | bytes 262160 | tf_op jit(solution)/shard_map/psum | solution.py:18
  762.2 1.7 broadcast_multiply_fusion
  763.9 1.1 copy.7
  764.9 1.0 fusion.7
  765.9 0.7 copy-done.7
  766.6 11.7 %cholesky.164 = f32[128,128]{1,0:T(8,128)S(1)} custom-call(f32[128,128]{1,0:T(8,128)S(1)} %cholesky.197), custom_call_target="Cholesky" | custom-call | tf_op jit(solution)/shard_map/jit(cholesky)/cholesky | solution.py:19
  778.4 9.8 %custom-call.15 = f32[1,128,128]{1,2,0:T(8,128)S(1)} custom-call(f32[1,128,128]{2,1,0:T(8,128)S(1)} %get-tuple-element.47), custom_call_target="InvertDiagBlocksLowerTriangular" | custom-call | tf_op jit(solution)/shard_map/jit(cholesky)/cholesky | solution.py:19
  788.2 1.0 constant_dynamic-update-slice_fusion.1
  789.3 1.1 convolution_subtract_fusion.2
  790.4 11.7 %cholesky.181 = f32[128,128]{1,0:T(8,128)S(1)} custom-call(f32[128,128]{1,0:T(8,128)S(1)} %convolution_subtract_fusion.2), custom_call_target="Cholesky" | custom-call | tf_op jit(solution)/shard_map/jit(cholesky)/cholesky | solution.py:19
  802.2 0.7 compare_reduce_fusion
  802.9 0.6 compare_reduce_fusion.1
  804.8 1.7 fusion.11
  806.6 4.3 while.5
  807.4 1.4 bitcast_dynamic-update-slice_fusion.5
  809.4 1.4 bitcast_dynamic-update-slice_fusion.5
  810.9 0.6 copy-done.8
  811.5 20.5 %custom-call.16 = f32[2,128,128]{1,2,0:T(8,128)S(1)} custom-call(f32[2,128,128]{2,1,0:T(8,128)} %copy-done.8), custom_call_target="InvertDiagBlocksLowerTriangular" | custom-call | tf_op jit(solution)/shard_map/jit(_solve_triangular)/triangular_solve | solution.py:20
  834.0 1.3 copy.8
  835.3 0.8 copy.9
  (48 shorter events, 5.4 us)
Async XLA Ops:
  7.2 1.6 copy-start
  7.2 61.8 %all-reduce.7.cloned.1.call-start = ((), (), s32[]{:S(2)}) async-start(), calls=%async_computation | async-start | bytes 2097152 | tf_op jit(solution)/shard_map/psum | solution.py:8
  15.5 235.8 %all-reduce.9.cloned.1.call-start = ((), (), s32[]{:S(2)}) async-start(), calls=%async_computation.1 | async-start | bytes 524288 | tf_op jit(solution)/shard_map/psum | solution.py:18
  69.0 250.2 %copy-start.1 = (f32[1024,256]{1,0:T(8,128)S(1)}, f32[1024,256]{1,0:T(8,128)}, u32[]{:S(2)}) copy-start(f32[1024,256]{1,0:T(8,128)} %all-reduce.7.cloned.1.call-done) | copy-start | bytes 3145732
  73.2 449.4 %all-reduce.11.cloned.1.call-start = ((), (), s32[]{:S(2)}) async-start(), calls=%async_computation.2 | async-start | bytes 8388608 | tf_op jit(solution)/shard_map/psum | solution.py:33
  255.0 0.7 copy-start.6
  291.2 2.0 copy-start.3
  330.9 249.6 %all-reduce.13.cloned.1.call-start = ((), (), s32[]{:S(2)}) async-start(), calls=%async_computation.3 | async-start | bytes 2097152 | tf_op jit(solution)/shard_map/psum | solution.py:8
  530.6 231.6 %all-reduce.15.cloned.1.call-start = ((), (), s32[]{:S(2)}) async-start(), calls=%async_computation.4 | async-start | bytes 524288 | tf_op jit(solution)/shard_map/psum | solution.py:18
  580.5 251.5 %copy-start.2 = (f32[1024,256]{0,1:T(8,128)S(1)}, f32[1024,256]{0,1:T(8,128)}, u32[]{:S(2)}) copy-start(f32[1024,256]{0,1:T(8,128)} %all-reduce.13.cloned.1.call-done) | copy-start | bytes 3145732
  765.9 0.7 copy-start.7
  802.1 2.7 copy-start.4
  810.9 0.7 copy-start.8
  833.3 2.1 copy-start.5
Sparse Core Ops, SparseCore 0:
  15.6 53.3 all-reduce.6
  73.5 177.7 all-reduce.8
  331.0 191.4 all-reduce.10
  530.7 49.7 all-reduce.12
  584.4 177.7 all-reduce.14
where the time goes:
time: 847 us; the launch traced here: 843 us
  waiting for transfers between devices  651 us (77%)
  other arithmetic  118 us (14%)
  matrix products  40 us (5%)
  between operations  16.9 us (2%)
  local copies, waits for them, and re-layouts  16.2 us (2%)
    psum x2, waiting for transfers between devices, orthonormal(): gram = lax.psum(gram_of(sketch), 'pos') / total  356 us
    psum x1, waiting for transfers between devices, per_device(): summed = lax.psum(loading_term, 'pos')  192 us
    psum x2, waiting for transfers between devices, pixel_total(): return lax.psum(partial_value, 'pix')  103 us
    another operation x13, other arithmetic, orthonormal(): lower = jnp.linalg.cholesky(gram)  68.7 us
    another operation x4, other arithmetic, orthonormal(): basis = jax.scipy.linalg.solve_triangular(lower, sketch.T, lower=True).T  41.8 us
  transfers between devices with their start and end apart: 5, of which 5 were waited for; matrix products, arithmetic and copies ran while one was open for 0% of the time, Pallas kernels for 0%

commit v1 on v0

v1 whole, which is shorter than its diff:
```python
import functools

import jax
import jax.numpy as jnp
from jax import lax
from jax.experimental import pallas as pl
from jax.experimental.pallas import tpu as pltpu
from jax.sharding import PartitionSpec as P

MESH = pl.DeviceIdType.MESH
F32 = jnp.float32
BF16 = jnp.bfloat16
HIGHEST = lax.Precision.HIGHEST
K = 256
ROWS = 256
LANES = 128
PANEL = 64

NT = (((1,), (1,)), ((), ()))
TN = (((0,), (0,)), ((), ()))


def dims_of(mesh):
    pos, pix = mesh.shape["pos"], mesh.shape["pix"]
    if pos == 64:
        return 4, 8, 2, pix
    return 2, pos // 4, 2, pix


def factor_panel(square):
    n = square.shape[0]
    at_row = lax.broadcasted_iota(jnp.int32, (n, n), 0)
    at_col = lax.broadcasted_iota(jnp.int32, (n, n), 1)
    eye = jnp.where(at_row == at_col, 1.0, 0.0).astype(F32)
    state = jnp.concatenate([square, eye], axis=1)
    rows = lax.broadcasted_iota(jnp.int32, (n, 1), 0)
    scale = jnp.zeros((n, 1), F32)
    for j in range(n):
        row = state[j : j + 1, :]
        pivot = state[j : j + 1, j : j + 1]
        below = jnp.where(rows > j, state[:, j : j + 1], 0.0)
        scale = jnp.where(rows == j, pivot, scale)
        state = state - (below / pivot) * row
    state = state * lax.rsqrt(scale)
    upper = jnp.where(at_col >= at_row, state[:, :n], 0.0)
    return upper, state[:, n:]


def factorise(work, size=K):
    for b in range(size // PANEL):
        lo, hi = b * PANEL, (b + 1) * PANEL
        upper, inverse = factor_panel(work[lo:hi, lo:hi])
        top = jnp.dot(inverse, work[lo:hi, :], precision=HIGHEST, preferred_element_type=F32)
        at_row = lax.broadcasted_iota(jnp.int32, top.shape, 0) + lo
        at_col = lax.broadcasted_iota(jnp.int32, top.shape, 1)
        top = jnp.where(at_col >= at_row, top, 0.0)
        work[lo:hi, :] = top
        if hi < size:
            work[hi:, :] -= lax.dot_general(
                top[:, hi:size], top, TN, precision=HIGHEST, preferred_element_type=F32
            )


def identity_beside(work, gram, size=K):
    at_row = lax.broadcasted_iota(jnp.int32, (size, size), 0)
    at_col = lax.broadcasted_iota(jnp.int32, (size, size), 1)
    work[:, :size] = gram
    work[:, size:] = jnp.where(at_row == at_col, 1.0, 0.0).astype(F32)


def sketch_kernel(
    dims,
    total,
    data_hbm,
    sketch_hbm,
    second_out,
    gram_out,
    data,
    sketch,
    send_a,
    recv_a,
    own_a,
    first_t,
    recv_c,
    own_c,
    send_x,
    recv_x,
    send_z,
    recv_z,
    own_z,
    pair,
    loads,
    acc,
    recv_d,
    parts,
    gsum,
    gathered,
    zparts,
    work,
    load_sem,
    sem_a,
    sem_f,
    sem_c,
    sem_x,
    sem_z,
    sem_p,
    sem_lz,
    sem_lx,
    sem_lc,
    sem_d,
    sem_s,
    sem_g1,
    sem_g2,
    sem_g3,
):
    nx, nz, nc, ny = dims
    half = K // nc
    quarter = nz * LANES
    pos, y = lax.axis_index("pos"), lax.axis_index("pix")
    x, z, c = pos // (nz * nc), lax.rem(pos // nc, nz), lax.rem(pos, nc)
    group = nx * ny * nc
    mine = (x * ny + y) * nc + c
    share = K // group

    def at(px, pz, pc, py):
        return ((px * nz + pz) * nc + pc, py)

    def ahead(i, o, n):
        return lax.rem(i + o, n)

    def member(i):
        return at(i // (ny * nc), z, lax.rem(i, nc), lax.rem(i // nc, ny))

    def remote(src, dst, send_sem, recv_sem, device):
        return pltpu.make_async_remote_copy(
            src_ref=src,
            dst_ref=dst,
            send_sem=send_sem,
            recv_sem=recv_sem,
            device_id=device,
            device_id_type=MESH,
        )

    def rows_of(i):
        return pl.ds(pl.multiple_of(i * ROWS, ROWS), ROWS)

    y_order = list(range(1, ny)) + [0]
    x_order = list(range(1, nx)) + [0]

    sketch_load = pltpu.make_async_copy(sketch_hbm, sketch, load_sem.at[ny])
    sketch_load.start()
    data_loads = []
    for o in y_order:
        rows = rows_of(ahead(y, o, ny))
        load = pltpu.make_async_copy(data_hbm.at[rows], data.at[rows], load_sem.at[o])
        load.start()
        data_loads.append(load)

    barrier = pltpu.get_barrier_semaphore()

    def greet_group(o, carry):
        pl.semaphore_signal(
            barrier, inc=1, device_id=member(ahead(mine, o, group)), device_id_type=MESH
        )
        return carry

    def greet_z(o, carry):
        pl.semaphore_signal(
            barrier, inc=1, device_id=at(x, ahead(z, o, nz), c, y), device_id_type=MESH
        )
        return carry

    lax.fori_loop(1, group, greet_group, 0)
    lax.fori_loop(1, nz, greet_z, 0)
    sketch_load.wait()

    copies_a = []
    for i, o in enumerate(y_order):
        data_loads[i].wait()
        block = jnp.dot(
            data[rows_of(ahead(y, o, ny)), :], sketch[...], preferred_element_type=F32
        )
        if o == 0:
            own_a[...] = block
        else:
            send_a[o - 1] = block.astype(BF16)
            if i == 0:
                pl.semaphore_wait(barrier, group - 1 + nz - 1)
            copy = remote(
                send_a.at[o - 1],
                recv_a.at[o - 1],
                sem_a.at[0, o - 1],
                sem_a.at[1, o - 1],
                at(x, z, c, ahead(y, o, ny)),
            )
            copy.start()
            copies_a.append(copy)
    first = own_a[...]
    for i, copy in enumerate(copies_a):
        copy.wait_recv()
        first = first + recv_a[i].astype(F32)
    mine_t = first.astype(BF16).T
    first_t[y] = mine_t
    copies_f = []
    for o in range(1, ny):
        copy = remote(
            first_t.at[y],
            first_t.at[y],
            sem_f.at[0, o - 1],
            sem_f.at[1, o - 1],
            at(x, z, c, ahead(y, o, ny)),
        )
        copy.start()
        copies_f.append(copy)

    def gram_scatter(n):
        def step(o, carry):
            to = ahead(mine, o, group)
            remote(
                gsum.at[n, to],
                parts.at[n, o],
                sem_g1.at[n, 0, o],
                sem_g1.at[n, 1, o],
                member(to),
            ).start()
            return carry

        lax.fori_loop(1, group, step, 0)

    def gram_across(n):
        def step(o, sums):
            remote(
                gsum.at[n, mine],
                parts.at[n, o],
                sem_g1.at[n, 0, o],
                sem_g1.at[n, 1, o],
                member(ahead(mine, o, group)),
            ).wait()
            return sums + parts[n, o]

        sums = lax.fori_loop(1, group, step, gsum[n, mine])
        zparts[n, 0] = sums

        def send(o, carry):
            remote(
                zparts.at[n, 0],
                zparts.at[n, o],
                sem_g2.at[n, 0, o],
                sem_g2.at[n, 1, o],
                at(x, ahead(z, o, nz), c, y),
            ).start()
            return carry

        lax.fori_loop(1, nz, send, 0)

    def gram_gather(n):
        def step(o, carry):
            remote(
                zparts.at[n, 0],
                zparts.at[n, o],
                sem_g2.at[n, 0, o],
                sem_g2.at[n, 1, o],
                at(x, ahead(z, o, nz), c, y),
            ).wait()
            return carry

        lax.fori_loop(1, nz, step, 0)

        def add(plane, sums):
            return sums + zparts[n, lax.rem(z - plane + nz, nz)]

        sums = lax.fori_loop(0, nz, add, jnp.zeros((share, K), F32))
        gathered[n, mine] = sums * (1.0 / total)

        def send(o, carry):
            remote(
                gathered.at[n, mine],
                gathered.at[n, mine],
                sem_g3.at[n, 0, o],
                sem_g3.at[n, 1, o],
                member(ahead(mine, o, group)),
            ).start()
            return carry

        lax.fori_loop(1, group, send, 0)

    def gram_done(n):
        def step(o, carry):
            remote(
                gathered.at[n, mine],
                gathered.at[n, lax.rem(mine - o + group, group)],
                sem_g3.at[n, 0, o],
                sem_g3.at[n, 1, o],
                member(ahead(mine, o, group)),
            ).wait()
            return carry

        lax.fori_loop(1, group, step, 0)
        return gathered[n].reshape(K, K)

    gsum[0] = lax.dot_general(mine_t, mine_t, NT, preferred_element_type=F32).reshape(
        group, share, K
    )
    gram_scatter(0)
    for copy in copies_f:
        copy.wait_recv()

    copies_c, copies_x = [], []
    for i, o in enumerate(x_order):
        xd = ahead(x, o, nx)

        def tile(t, carry):
            cols = pl.ds(pl.multiple_of(xd * quarter + t * ROWS, ROWS), ROWS)
            here = pl.ds(pl.multiple_of(t * ROWS, ROWS), ROWS)
            block = jnp.zeros((K, ROWS), F32)
            for q in range(ny):
                block += jnp.dot(
                    first_t[q], data[q * ROWS : (q + 1) * ROWS, cols], preferred_element_type=F32
                )
            own_c[i, :, :, here] = block.reshape(nc, half, ROWS)
            return carry

        lax.fori_loop(0, quarter // ROWS, tile, 0)
        copy = remote(
            own_c.at[i, 1 - c],
            recv_c.at[i],
            sem_c.at[0, i],
            sem_c.at[1, i],
            at(x, z, 1 - c, y),
        )
        copy.start()
        copies_c.append(copy)
        if i == 0:
            gram_across(0)
        if i > 0:
            j = i - 1
            copies_c[j].wait_recv()
            send_x[j] = (own_c[j, c] + recv_c[j]).astype(BF16)
            copy = remote(
                send_x.at[j],
                recv_x.at[j],
                sem_x.at[0, j],
                sem_x.at[1, j],
                at(ahead(x, x_order[j], nx), z, c, y),
            )
            copy.start()
            copies_x.append(copy)
    gram_gather(0)

    identity_beside(work, gram_done(0))
    factorise(work)

    last = nx - 1
    copies_c[last].wait_recv()
    for copy in copies_x:
        copy.wait_recv()
    copies_z = []
    for o in list(range(1, nz)) + [0]:
        zd = ahead(z, o, nz)
        cols = pl.ds(pl.multiple_of(zd * LANES, LANES), LANES)
        block = own_c[last, c, :, cols] + recv_c[last, :, cols]
        for j in range(nx - 1):
            block = block + recv_x[j, :, cols].astype(F32)
        if o == 0:
            own_z[...] = block
        else:
            send_z[o - 1] = block.astype(BF16)
            copy = remote(
                send_z.at[o - 1],
                recv_z.at[o - 1],
                sem_z.at[0, o - 1],
                sem_z.at[1, o - 1],
                at(x, zd, c, y),
            )
            copy.start()
            copies_z.append(copy)
    block = own_z[...]
    for j, copy in enumerate(copies_z):
        copy.wait_recv()
        block = block + recv_z[j].astype(F32)
    pair[c] = block
    copy_p = remote(pair.at[c], pair.at[c], sem_p.at[0], sem_p.at[1], at(x, z, 1 - c, y))
    copy_p.start()
    copy_p.wait_recv()

    own_rows = pl.ds(pl.multiple_of(c * half, half), half)
    solved = jnp.dot(
        work[own_rows, K:],
        pair[...].reshape(K, LANES),
        precision=HIGHEST,
        preferred_element_type=F32,
    )

    def cell(px, pz, pc):
        cols = pl.ds(pl.multiple_of((px * nz + pz) * LANES, LANES), LANES)
        return loads.at[pl.ds(pl.multiple_of(pc * half, half), half), cols]

    cell(x, z, c)[...] = (solved * (1.0 / total)).astype(BF16)

    def over_z(o):
        return remote(
            cell(x, z, c),
            cell(x, z, c),
            sem_lz.at[0, o],
            sem_lz.at[1, o],
            at(x, ahead(z, o, nz), c, y),
        )

    def over_x(ox, oz):
        this = cell(x, lax.rem(z - oz + nz, nz), c)
        return remote(
            this, this, sem_lx.at[0, ox, oz], sem_lx.at[1, ox, oz], at(ahead(x, ox, nx), z, c, y)
        )

    def over_c(ox, oz):
        this = cell(lax.rem(x - ox + nx, nx), lax.rem(z - oz + nz, nz), c)
        return remote(
            this, this, sem_lc.at[0, ox, oz], sem_lc.at[1, ox, oz], at(x, z, 1 - c, y)
        )

    for o in range(1, nz):
        over_z(o).start()

    def forward(oz, carry):
        @pl.when(oz > 0)
        def _():
            over_z(oz).wait_recv()

        for ox in range(1, nx):
            over_x(ox, oz).start()
        over_c(0, oz).start()
        return carry

    lax.fori_loop(0, nz, forward, 0)

    for ox in range(nx):
        def pass_on(oz, carry):
            over_x(ox, oz).wait_recv()
            over_c(ox, oz).start()
            return carry

        def arrived(oz, carry):
            over_c(ox, oz).wait_recv()
            return carry

        if ox > 0:
            lax.fori_loop(0, nz, pass_on, 0)
        lax.fori_loop(0, nz, arrived, 0)
        cols = pl.ds(
            pl.multiple_of(lax.rem(x - ox + nx, nx) * quarter, quarter), quarter
        )
        copies_d = []
        for o in y_order:
            rows = rows_of(ahead(y, o, ny))
            term = lax.dot_general(data[rows, cols], loads[:, cols], NT, preferred_element_type=F32)
            if ox == 0:
                acc[o] = term
            else:
                acc[o] += term
            if ox == nx - 1 and o > 0:
                copy = remote(
                    acc.at[o],
                    recv_d.at[o - 1],
                    sem_d.at[0, o - 1],
                    sem_d.at[1, o - 1],
                    at(x, z, c, ahead(y, o, ny)),
                )
                copy.start()
                copies_d.append(copy)
    second = acc[0]
    for j, copy in enumerate(copies_d):
        copy.wait_recv()
        second = second + recv_d[j]
    second_out[y] = second

    gsum[1] = lax.dot_general(
        second, second, TN, precision=HIGHEST, preferred_element_type=F32
    ).reshape(group, share, K)
    gram_scatter(1)
    copies_s = []
    for o in range(1, ny):
        copy = remote(
            second_out.at[y],
            second_out.at[y],
            sem_s.at[0, o - 1],
            sem_s.at[1, o - 1],
            at(x, z, c, ahead(y, o, ny)),
        )
        copy.start()
        copies_s.append(copy)
    gram_across(1)
    gram_gather(1)
    gram_out[...] = gram_done(1)

    for copy in copies_s:
        copy.wait()
    for copy in copies_a + copies_f + copies_c + copies_x + copies_z + copies_d + [copy_p]:
        copy.wait_send()

    def drain(oz, carry):
        for ox in range(1, nx):
            over_x(ox, oz).wait_send()
        for ox in range(nx):
            over_c(ox, oz).wait_send()
        return carry

    def drain_z(oz, carry):
        over_z(oz).wait_send()
        return carry

    lax.fori_loop(0, nz, drain, 0)
    lax.fori_loop(1, nz, drain_z, 0)


def basis_kernel(second, gram, basis, factor, work):
    identity_beside(work, gram[...])
    factorise(work)
    factor[...] = work[:, :K]
    inverse = work[:, K:]
    for q in range(second.shape[0] // ROWS):
        rows = pl.ds(q * ROWS, ROWS)
        basis[rows, :] = lax.dot_general(
            second[rows, :], inverse, NT, precision=HIGHEST, preferred_element_type=F32
        )


def per_device(dims, data, sketch_matrix):
    nx, nz, nc, ny = dims
    rows, pixels = data.shape
    total = rows * nx * nz * nc
    half, quarter, group = K // nc, nz * LANES, nx * ny * nc
    share = K // group
    assert rows == ny * ROWS and pixels == nx * quarter
    vm = pltpu.VMEM
    dma = pltpu.SemaphoreType.DMA
    second, gram = pl.pallas_call(
        functools.partial(sketch_kernel, dims, total),
        out_shape=(
            jax.ShapeDtypeStruct((ny, ROWS, K), F32),
            jax.ShapeDtypeStruct((K, K), F32),
        ),
        in_specs=[pl.BlockSpec(memory_space=pl.ANY)] * 2,
        out_specs=(pl.BlockSpec(memory_space=pltpu.VMEM),) * 2,
        scratch_shapes=[
            vm((rows, pixels), BF16),
            vm((pixels, K), BF16),
            vm((ny - 1, ROWS, K), BF16),
            vm((ny - 1, ROWS, K), BF16),
            vm((ROWS, K), F32),
            vm((ny, K, ROWS), BF16),
            vm((nx, half, quarter), F32),
            vm((nx, nc, half, quarter), F32),
            vm((nx - 1, half, quarter), BF16),
            vm((nx - 1, half, quarter), BF16),
            vm((nz - 1, half, LANES), BF16),
            vm((nz - 1, half, LANES), BF16),
            vm((half, LANES), F32),
            vm((nc, half, LANES), F32),
            vm((K, pixels), BF16),
            vm((ny, ROWS, K), F32),
            vm((ny - 1, ROWS, K), F32),
            vm((2, group, share, K), F32),
            vm((2, group, share, K), F32),
            vm((2, group, share, K), F32),
            vm((2, nz, share, K), F32),
            vm((K, 2 * K), F32),
            dma((ny + 1,)),
            dma((2, ny - 1)),
            dma((2, ny - 1)),
            dma((2, nx)),
            dma((2, nx - 1)),
            dma((2, nz - 1)),
            dma((2,)),
            dma((2, nz)),
            dma((2, nx, nz)),
            dma((2, nx, nz)),
            dma((2, ny - 1)),
            dma((2, ny - 1)),
            dma((2, 2, group)),
            dma((2, 2, nz)),
            dma((2, 2, group)),
        ],
        compiler_params=pltpu.CompilerParams(
            collective_id=0, has_side_effects=True, vmem_limit_bytes=50 * 1024 * 1024
        ),
        cost_estimate=pl.CostEstimate(
            flops=6 * rows * pixels * K, bytes_accessed=2 * rows * pixels, transcendentals=0
        ),
        name="sketch",
    )(data, sketch_matrix)
    basis, factor = pl.pallas_call(
        basis_kernel,
        out_shape=(
            jax.ShapeDtypeStruct((rows, K), F32),
            jax.ShapeDtypeStruct((K, K), F32),
        ),
        in_specs=[pl.BlockSpec(memory_space=pltpu.VMEM)] * 2,
        out_specs=(pl.BlockSpec(memory_space=pltpu.VMEM),) * 2,
        scratch_shapes=[pltpu.VMEM((K, 2 * K), F32)],
        compiler_params=pltpu.CompilerParams(vmem_limit_bytes=32 * 1024 * 1024),
        name="basis",
    )(second.reshape(rows, K), gram)
    return basis, factor


def solution(mesh):
    in_specs = (P("pos", "pix"), P("pix", None))
    out_specs = (P("pos", None), P())
    return jax.shard_map(
        functools.partial(per_device, dims_of(mesh)),
        mesh=mesh,
        in_specs=in_specs,
        out_specs=out_specs,
        check_vma=False,
    )
```

time: 847 us -> 183 us (0.22)
  waiting for transfers between devices: 651 us -> 0 us
  Pallas kernels: 0 us -> 181 us
  other arithmetic: 118 us -> 0 us
  matrix products: 40 us -> 0 us
  between operations: 16.9 us -> 0.65 us
  local copies, waits for them, and re-layouts: 16.2 us -> 1.58 us
    psum x5 -> x0, waiting for transfers between devices: 651 us -> none  [the longest x2 356 us: orthonormal(): gram = lax.psum(gram_of(sketch), 'pos') / total]
    pallas_call x0 -> x2, Pallas kernels: none -> 181 us  [the longest x1 152 us: per_device(): pl.pallas_call(functools.partial(sketch_kernel, dims, total), out_shape=(...]
    another operation x17 -> x0, other arithmetic: 110 us -> none  [the longest x13 68.7 us: orthonormal(): lower = jnp.linalg.cholesky(gram)]
    dot_general x5 -> x0, matrix products: 29.9 us -> none  [the longest x1 7.99 us: per_device(): partial_value = jnp.dot(data, loads, preferred_element_type=jnp.float32)]
    another operation x10 -> x0, matrix products: 10.1 us -> none  [the longest x6 5.82 us: orthonormal(): basis = jax.scipy.linalg.solve_triangular(lower, sketch.T, lower=True).T]
  transfers between devices with their start and end apart: 5 -> 0, of which waited for: 5 -> 0; matrix products, arithmetic and copies ran while one was open for 0% -> 0% of each run, Pallas kernels for 0% -> 0%
where the time goes in v1:
time: 183 us
  Pallas kernels  181 us (99%)
    pallas_call x1, Pallas kernels, per_device(): pl.pallas_call(functools.partial(sketch_kernel, dims, total), out_shape=(...  152 us
    pallas_call x1, Pallas kernels, per_device(): pl.pallas_call(basis_kernel, out_shape=(jax.ShapeDtypeStruct((rows, K), F...  28.8 us

profile of v1, /device:TPU:1, one launch (start us, length us, event | category | flops | bytes accessed | tf_op | source)
XLA Modules:
  0.0 183.3 jit_solution(14593805603458056060)
XLA Ops:
  0.6 0.0 copy-start
  0.6 1.6 copy-done
  2.2 152.3 %sketch.1 = (f32[4,256,256]{2,1,0:T(8,128)S(1)}, f32[256,256]{1,0:T(8,128)S(1)}) custom-call(bf16[1024,4096]{1,0:T(8,128)(2,1)} %data_hbm.1, bf16[4096,256]{1,0:T(8,128)(2,1)S(1)} %copy-done), custom_call_target="tpu_custom_call" | custom-call | flops 6442450944 | bytes 8388608 | tf_op jit(solution)/shard_map/sketch/pallas_call | solution.py:536
  154.5 28.8 %basis.1 = (f32[1024,256]{1,0:T(8,128)}, f32[256,256]{1,0:T(8,128)}) custom-call(f32[1024,256]{1,0:T(8,128)S(1)} %bitcast.1, f32[256,256]{1,0:T(8,128)S(1)} %get-tuple-element.5.gram), custom_call_target="tpu_custom_call" | custom-call | tf_op jit(solution)/shard_map/basis/pallas_call | solution.py:591
Async XLA Ops:
  0.6 1.6 copy-start

commit v2 on v1

--- a/solution.py
+++ b/solution.py
@@ -15,6 +15,7 @@
 ROWS = 256
 LANES = 128
 PANEL = 64
+SUB = 8
 
 NT = (((1,), (1,)), ((), ()))
 TN = (((0,), (0,)), ((), ()))
@@ -22,9 +23,12 @@
 
 def dims_of(mesh):
     pos, pix = mesh.shape["pos"], mesh.shape["pix"]
-    if pos == 64:
-        return 4, 8, 2, pix
-    return 2, pos // 4, 2, pix
+    nx = 4 if pos >= 16 else 2
+    return nx, pos // (2 * nx), 2, pix
+
+
+def spread(column):
+    return jnp.broadcast_to(column, (SUB, 2 * PANEL))
 
 
 def factor_panel(square):
@@ -33,17 +37,37 @@
     at_col = lax.broadcasted_iota(jnp.int32, (n, n), 1)
     eye = jnp.where(at_row == at_col, 1.0, 0.0).astype(F32)
     state = jnp.concatenate([square, eye], axis=1)
-    rows = lax.broadcasted_iota(jnp.int32, (n, 1), 0)
-    scale = jnp.zeros((n, 1), F32)
-    for j in range(n):
-        row = state[j : j + 1, :]
-        pivot = state[j : j + 1, j : j + 1]
-        below = jnp.where(rows > j, state[:, j : j + 1], 0.0)
-        scale = jnp.where(rows == j, pivot, scale)
-        state = state - (below / pivot) * row
-    state = state * lax.rsqrt(scale)
-    upper = jnp.where(at_col >= at_row, state[:, :n], 0.0)
-    return upper, state[:, n:]
+    groups = n // SUB
+    rows = [state[SUB * g : SUB * (g + 1), :] for g in range(groups)]
+    sub = lax.broadcasted_iota(jnp.int32, (SUB, 2 * n), 0)
+    lane = lax.broadcasted_iota(jnp.int32, (SUB, 2 * n), 1)
+    done = []
+    for g in range(groups):
+        at = SUB * g
+        cols = {
+            h: [spread(rows[h][:, at + k : at + k + 1]) for k in range(SUB)]
+            for h in range(g, groups)
+        }
+        top, panel = rows[g], cols[g]
+        pivots = jnp.ones((SUB, 2 * n), F32)
+        for j in range(SUB):
+            pivot = panel[j][j : j + 1, :]
+            inverse = 1.0 / pivot
+            pivots = jnp.where(sub == j, pivot, pivots)
+            heads = [panel[k][j : j + 1, :] for k in range(SUB)]
+            row = top[j : j + 1, :]
+            below = jnp.where(sub > j, panel[j], 0.0) * inverse
+            for k in range(j + 1, SUB):
+                panel[k] = panel[k] - below * heads[k]
+            top = top - below * row
+            for h in range(g + 1, groups):
+                scaled = cols[h][j] * inverse
+                for k in range(j + 1, SUB):
+                    cols[h][k] = cols[h][k] - scaled * heads[k]
+                rows[h] = rows[h] - scaled * row
+        done.append(jnp.where(lane >= sub + at, top * lax.rsqrt(pivots), 0.0))
+    state = jnp.concatenate(done, axis=0)
+    return state[:, :n], state[:, n:]
 
 
 def factorise(work, size=K):
@@ -73,8 +97,8 @@
     total,
     data_hbm,
     sketch_hbm,
-    second_out,
-    gram_out,
+    basis_out,
+    factor_out,
     data,
     sketch,
     send_a,
@@ -92,6 +116,9 @@
     loads,
     acc,
     recv_d,
+    send_far,
+    recv_far,
+    second,
     parts,
     gsum,
     gathered,
@@ -144,8 +171,11 @@
     def rows_of(i):
         return pl.ds(pl.multiple_of(i * ROWS, ROWS), ROWS)
 
-    y_order = list(range(1, ny)) + [0]
-    x_order = list(range(1, nx)) + [0]
+    def by_distance(n):
+        return sorted(range(1, n), key=lambda o: (-min(o, n - o), o)) + [0]
+
+    y_order, x_order, z_order = by_distance(ny), by_distance(nx), by_distance(nz)
+    near_first = z_order[::-1]
 
     sketch_load = pltpu.make_async_copy(sketch_hbm, sketch, load_sem.at[ny])
     sketch_load.start()
@@ -196,13 +226,14 @@
             copy.start()
             copies_a.append(copy)
     first = own_a[...]
-    for i, copy in enumerate(copies_a):
+    for copy in copies_a:
         copy.wait_recv()
-        first = first + recv_a[i].astype(F32)
+    for o in range(1, ny):
+        first = first + recv_a[o - 1].astype(F32)
     mine_t = first.astype(BF16).T
     first_t[y] = mine_t
-    copies_f = []
-    for o in range(1, ny):
+    copies_f = {}
+    for o in y_order[:-1]:
         copy = remote(
             first_t.at[y],
             first_t.at[y],
@@ -211,7 +242,7 @@
             at(x, z, c, ahead(y, o, ny)),
         )
         copy.start()
-        copies_f.append(copy)
+        copies_f[o] = copy
 
     def gram_scatter(n):
         def step(o, carry):
@@ -302,25 +333,35 @@
         group, share, K
     )
     gram_scatter(0)
-    for copy in copies_f:
-        copy.wait_recv()
-
-    copies_c, copies_x = [], []
-    for i, o in enumerate(x_order):
-        xd = ahead(x, o, nx)
+
+    def add_rows(o, i):
+        block_at = lax.rem(y - o + ny, ny)
+        xd = ahead(x, x_order[i], nx)
 
         def tile(t, carry):
             cols = pl.ds(pl.multiple_of(xd * quarter + t * ROWS, ROWS), ROWS)
             here = pl.ds(pl.multiple_of(t * ROWS, ROWS), ROWS)
-            block = jnp.zeros((K, ROWS), F32)
-            for q in range(ny):
-                block += jnp.dot(
-                    first_t[q], data[q * ROWS : (q + 1) * ROWS, cols], preferred_element_type=F32
-                )
-            own_c[i, :, :, here] = block.reshape(nc, half, ROWS)
+            block = jnp.dot(
+                first_t[block_at], data[rows_of(block_at), cols], preferred_element_type=F32
+            ).reshape(nc, half, ROWS)
+            if o == 0:
+                own_c[i, :, :, here] = block
+            else:
+                own_c[i, :, :, here] += block
             return carry
 
         lax.fori_loop(0, quarter // ROWS, tile, 0)
+
+    arrivals = y_order[::-1]
+    for o in arrivals[:-1]:
+        if o > 0:
+            copies_f[o].wait_recv()
+        for i in range(nx):
+            add_rows(o, i)
+    copies_f[arrivals[-1]].wait_recv()
+    copies_c, copies_x = [], []
+    for i in range(nx):
+        add_rows(arrivals[-1], i)
         copy = remote(
             own_c.at[i, 1 - c],
             recv_c.at[i],
@@ -330,32 +371,26 @@
         )
         copy.start()
         copies_c.append(copy)
-        if i == 0:
-            gram_across(0)
-        if i > 0:
-            j = i - 1
-            copies_c[j].wait_recv()
-            send_x[j] = (own_c[j, c] + recv_c[j]).astype(BF16)
-            copy = remote(
-                send_x.at[j],
-                recv_x.at[j],
-                sem_x.at[0, j],
-                sem_x.at[1, j],
-                at(ahead(x, x_order[j], nx), z, c, y),
-            )
-            copy.start()
-            copies_x.append(copy)
+    gram_across(0)
+    for i in range(nx - 1):
+        copies_c[i].wait_recv()
+        send_x[i] = (own_c[i, c] + recv_c[i]).astype(BF16)
+        copy = remote(
+            send_x.at[i],
+            recv_x.at[i],
+            sem_x.at[0, i],
+            sem_x.at[1, i],
+            at(ahead(x, x_order[i], nx), z, c, y),
+        )
+        copy.start()
+        copies_x.append(copy)
     gram_gather(0)
-
-    identity_beside(work, gram_done(0))
-    factorise(work)
-
     last = nx - 1
     copies_c[last].wait_recv()
     for copy in copies_x:
         copy.wait_recv()
     copies_z = []
-    for o in list(range(1, nz)) + [0]:
+    for o in z_order:
         zd = ahead(z, o, nz)
         cols = pl.ds(pl.multiple_of(zd * LANES, LANES), LANES)
         block = own_c[last, c, :, cols] + recv_c[last, :, cols]
@@ -374,9 +409,14 @@
             )
             copy.start()
             copies_z.append(copy)
+
+    identity_beside(work, gram_done(0))
+    factorise(work)
+
     block = own_z[...]
-    for j, copy in enumerate(copies_z):
+    for copy in copies_z:
         copy.wait_recv()
+    for j in range(nz - 1):
         block = block + recv_z[j].astype(F32)
     pair[c] = block
     copy_p = remote(pair.at[c], pair.at[c], sem_p.at[0], sem_p.at[1], at(x, z, 1 - c, y))
@@ -406,10 +446,14 @@
             at(x, ahead(z, o, nz), c, y),
         )
 
-    def over_x(ox, oz):
-        this = cell(x, lax.rem(z - oz + nz, nz), c)
+    def over_x(ox, oz, hops):
+        this = cell(lax.rem(x - ox + hops + nx, nx), lax.rem(z - oz + nz, nz), c)
         return remote(
-            this, this, sem_lx.at[0, ox, oz], sem_lx.at[1, ox, oz], at(ahead(x, ox, nx), z, c, y)
+            this,
+            this,
+            sem_lx.at[0, ox, oz],
+            sem_lx.at[1, ox, oz],
+            at(lax.rem(x + hops + nx, nx), z, c, y),
         )
 
     def over_c(ox, oz):
@@ -418,110 +462,115 @@
             this, this, sem_lc.at[0, ox, oz], sem_lc.at[1, ox, oz], at(x, z, 1 - c, y)
         )
 
-    for o in range(1, nz):
+    for o in z_order[:-1]:
         over_z(o).start()
-
-    def forward(oz, carry):
-        @pl.when(oz > 0)
-        def _():
-            over_z(oz).wait_recv()
-
-        for ox in range(1, nx):
-            over_x(ox, oz).start()
-        over_c(0, oz).start()
-        return carry
-
-    lax.fori_loop(0, nz, forward, 0)
-
-    for ox in range(nx):
-        def pass_on(oz, carry):
-            over_x(ox, oz).wait_recv()
-            over_c(ox, oz).start()
-            return carry
-
-        def arrived(oz, carry):
+    steps = list(near_first)
+    copies_lx = []
+
+    def start_x(ox, oz, hops):
+        copy = over_x(ox, oz, hops)
+        copy.start()
+        copies_lx.append(copy)
+
+    for n in range(nz + 2):
+        if n < nz:
+            oz = steps[n]
+            if oz > 0:
+                over_z(oz).wait_recv()
+            start_x(1, oz, 1)
+            if nx > 2:
+                start_x(nx - 1, oz, -1)
+            over_c(0, oz).start()
+        if n >= 2:
+            oz = steps[n - 2]
+            over_x(1, oz, 1).wait_recv()
+            if nx == 4 and n % 2 == 0:
+                start_x(2, oz, 1)
+            over_c(1, oz).start()
+            if nx == 4:
+                over_x(3, oz, -1).wait_recv()
+                if n % 2 == 1:
+                    start_x(2, oz, -1)
+                over_c(3, oz).start()
+
+    def add_pixels(ox):
+        for oz in steps:
             over_c(ox, oz).wait_recv()
-            return carry
-
-        if ox > 0:
-            lax.fori_loop(0, nz, pass_on, 0)
-        lax.fori_loop(0, nz, arrived, 0)
         cols = pl.ds(
             pl.multiple_of(lax.rem(x - ox + nx, nx) * quarter, quarter), quarter
         )
-        copies_d = []
+        copies = []
         for o in y_order:
             rows = rows_of(ahead(y, o, ny))
             term = lax.dot_general(data[rows, cols], loads[:, cols], NT, preferred_element_type=F32)
-            if ox == 0:
+            if ox > 0:
+                term = acc[o] + term
+            if ox != nx // 2 or 2 * o != ny:
                 acc[o] = term
-            else:
-                acc[o] += term
-            if ox == nx - 1 and o > 0:
+            if ox == nx // 2 and o > 0:
+                if 2 * o == ny:
+                    send_far[...] = term.astype(BF16)
                 copy = remote(
-                    acc.at[o],
-                    recv_d.at[o - 1],
+                    send_far if 2 * o == ny else acc.at[o],
+                    recv_far if 2 * o == ny else recv_d.at[o - 1],
                     sem_d.at[0, o - 1],
                     sem_d.at[1, o - 1],
                     at(x, z, c, ahead(y, o, ny)),
                 )
                 copy.start()
-                copies_d.append(copy)
-    second = acc[0]
-    for j, copy in enumerate(copies_d):
+                copies.append(copy)
+        return copies
+
+    add_pixels(0)
+    if nx == 4:
+        for n, oz in enumerate(steps):
+            over_x(2, oz, 1 if n % 2 == 0 else -1).wait_recv()
+            over_c(2, oz).start()
+        add_pixels(1)
+        add_pixels(3)
+    copies_d = add_pixels(nx // 2)
+    mine_s = acc[0]
+    for copy in copies_d:
         copy.wait_recv()
-        second = second + recv_d[j]
-    second_out[y] = second
+    for o in range(1, ny):
+        mine_s = mine_s + (recv_far[...].astype(F32) if 2 * o == ny else recv_d[o - 1])
+    second[y] = mine_s
 
     gsum[1] = lax.dot_general(
-        second, second, TN, precision=HIGHEST, preferred_element_type=F32
+        mine_s, mine_s, TN, precision=HIGHEST, preferred_element_type=F32
     ).reshape(group, share, K)
     gram_scatter(1)
+    gram_across(1)
+    gram_gather(1)
     copies_s = []
-    for o in range(1, ny):
+    for o in y_order[:-1]:
         copy = remote(
-            second_out.at[y],
-            second_out.at[y],
+            second.at[y],
+            second.at[y],
             sem_s.at[0, o - 1],
             sem_s.at[1, o - 1],
             at(x, z, c, ahead(y, o, ny)),
         )
         copy.start()
         copies_s.append(copy)
-    gram_across(1)
-    gram_gather(1)
-    gram_out[...] = gram_done(1)
-
+    identity_beside(work, gram_done(1))
+    factorise(work)
+    factor_out[...] = work[:, :K]
     for copy in copies_s:
         copy.wait()
-    for copy in copies_a + copies_f + copies_c + copies_x + copies_z + copies_d + [copy_p]:
+    for q in range(ny):
+        basis_out[q * ROWS : (q + 1) * ROWS, :] = lax.dot_general(
+            second[q], work[:, K:], NT, precision=HIGHEST, preferred_element_type=F32
+        )
+
+    copies = copies_a + list(copies_f.values()) + copies_c + copies_x + copies_z + copies_d
+    for copy in copies + copies_lx + [copy_p]:
         copy.wait_send()
-
-    def drain(oz, carry):
-        for ox in range(1, nx):
-            over_x(ox, oz).wait_send()
+    for oz in range(nz):
+        if oz > 0:
+            over_z(oz).wait_send()
         for ox in range(nx):
             over_c(ox, oz).wait_send()
-        return carry
-
-    def drain_z(oz, carry):
-        over_z(oz).wait_send()
-        return carry
-
-    lax.fori_loop(0, nz, drain, 0)
-    lax.fori_loop(1, nz, drain_z, 0)
-
-
-def basis_kernel(second, gram, basis, factor, work):
-    identity_beside(work, gram[...])
-    factorise(work)
-    factor[...] = work[:, :K]
-    inverse = work[:, K:]
-    for q in range(second.shape[0] // ROWS):
-        rows = pl.ds(q * ROWS, ROWS)
-        basis[rows, :] = lax.dot_general(
-            second[rows, :], inverse, NT, precision=HIGHEST, preferred_element_type=F32
-        )
 
 
 def per_device(dims, data, sketch_matrix):
@@ -533,10 +582,10 @@
     assert rows == ny * ROWS and pixels == nx * quarter
     vm = pltpu.VMEM
     dma = pltpu.SemaphoreType.DMA
-    second, gram = pl.pallas_call(
+    return pl.pallas_call(
         functools.partial(sketch_kernel, dims, total),
         out_shape=(
-            jax.ShapeDtypeStruct((ny, ROWS, K), F32),
+            jax.ShapeDtypeStruct((rows, K), F32),
             jax.ShapeDtypeStruct((K, K), F32),
         ),
         in_specs=[pl.BlockSpec(memory_space=pl.ANY)] * 2,
@@ -559,6 +608,9 @@
             vm((K, pixels), BF16),
             vm((ny, ROWS, K), F32),
             vm((ny - 1, ROWS, K), F32),
+            vm((ROWS, K), BF16),
+            vm((ROWS, K), BF16),
+            vm((ny, ROWS, K), F32),
             vm((2, group, share, K), F32),
             vm((2, group, share, K), F32),
             vm((2, group, share, K), F32),
@@ -581,26 +633,13 @@
             dma((2, 2, group)),
         ],
         compiler_params=pltpu.CompilerParams(
-            collective_id=0, has_side_effects=True, vmem_limit_bytes=50 * 1024 * 1024
+            collective_id=0, has_side_effects=True, vmem_limit_bytes=60 * 1024 * 1024
         ),
         cost_estimate=pl.CostEstimate(
             flops=6 * rows * pixels * K, bytes_accessed=2 * rows * pixels, transcendentals=0
         ),
         name="sketch",
     )(data, sketch_matrix)
-    basis, factor = pl.pallas_call(
-        basis_kernel,
-        out_shape=(
-            jax.ShapeDtypeStruct((rows, K), F32),
-            jax.ShapeDtypeStruct((K, K), F32),
-        ),
-        in_specs=[pl.BlockSpec(memory_space=pltpu.VMEM)] * 2,
-        out_specs=(pl.BlockSpec(memory_space=pltpu.VMEM),) * 2,
-        scratch_shapes=[pltpu.VMEM((K, 2 * K), F32)],
-        compiler_params=pltpu.CompilerParams(vmem_limit_bytes=32 * 1024 * 1024),
-        name="basis",
-    )(second.reshape(rows, K), gram)
-    return basis, factor
 
 
 def solution(mesh):

time: 183 us -> 146 us (0.80)
  Pallas kernels: 181 us -> 142 us
  local copies, waits for them, and re-layouts: 1.58 us -> 3.93 us
    pallas_call x1 -> x0, Pallas kernels: 28.8 us -> none  [per_device(): pl.pallas_call(basis_kernel, out_shape=(jax.ShapeDtypeStruct((rows, K), F...]
    pallas_call x1, Pallas kernels: 152 us -> 142 us  [per_device(): pl.pallas_call(functools.partial(sketch_kernel, dims, total), out_shape=(...]
    unnamed x2, local copies, waits for them, and re-layouts: 1.58 us -> 3.93 us
where the time goes in v2:
time: 146 us
  Pallas kernels  142 us (97%)
  local copies, waits for them, and re-layouts  3.93 us (3%)
    pallas_call x1, Pallas kernels, per_device(): pl.pallas_call(functools.partial(sketch_kernel, dims, total), out_shape=(...  142 us
    unnamed x2, local copies, waits for them, and re-layouts  3.93 us

profile of v2, /device:TPU:1, one launch (start us, length us, event | category | flops | bytes accessed | tf_op | source)
XLA Modules:
  0.0 146.1 jit_solution(1508438305097102863)
XLA Ops:
  0.6 141.6 %sketch.1 = (f32[1024,256]{1,0:T(8,128)}, f32[256,256]{1,0:T(8,128)}) custom-call(bf16[1024,4096]{1,0:T(8,128)(2,1)} %data_hbm.1, bf16[4096,256]{1,0:T(8,128)(2,1)} %sketch_hbm.1), custom_call_target="tpu_custom_call" | custom-call | flops 6442450944 | bytes 8388608 | tf_op jit(solution)/shard_map/sketch/pallas_call | solution.py:585
  142.2 2.3 %copy.6 = f32[1024,256]{1,0:T(8,128)} copy(f32[1024,256]{1,0:T(8,128)} %get-tuple-element.4) | data formatting | bytes 2097152
  144.5 1.7 %copy.7 = f32[256,256]{1,0:T(8,128)} copy(f32[256,256]{1,0:T(8,128)} %get-tuple-element.5) | data formatting | bytes 524288

commit v3 on v2

--- a/solution.py
+++ b/solution.py
@@ -15,6 +15,7 @@
 ROWS = 256
 LANES = 128
 PANEL = 64
+PANELS = range(K // PANEL)
 SUB = 8
 
 NT = (((1,), (1,)), ((), ()))
@@ -70,8 +71,8 @@
     return state[:, :n], state[:, n:]
 
 
-def factorise(work, size=K):
-    for b in range(size // PANEL):
+def factorise(work, panels, size=K):
+    for b in panels:
         lo, hi = b * PANEL, (b + 1) * PANEL
         upper, inverse = factor_panel(work[lo:hi, lo:hi])
         top = jnp.dot(inverse, work[lo:hi, :], precision=HIGHEST, preferred_element_type=F32)
@@ -97,8 +98,8 @@
     total,
     data_hbm,
     sketch_hbm,
-    basis_out,
-    factor_out,
+    second_out,
+    work_out,
     data,
     sketch,
     send_a,
@@ -118,7 +119,6 @@
     recv_d,
     send_far,
     recv_far,
-    second,
     parts,
     gsum,
     gathered,
@@ -136,9 +136,7 @@
     sem_lc,
     sem_d,
     sem_s,
-    sem_g1,
-    sem_g2,
-    sem_g3,
+    sem_g,
 ):
     nx, nz, nc, ny = dims
     half = K // nc
@@ -244,14 +242,17 @@
         copy.start()
         copies_f[o] = copy
 
+    def wait_all(ref, sem):
+        pltpu.make_async_copy(ref, ref, sem).wait()
+
     def gram_scatter(n):
         def step(o, carry):
             to = ahead(mine, o, group)
             remote(
                 gsum.at[n, to],
-                parts.at[n, o],
-                sem_g1.at[n, 0, o],
-                sem_g1.at[n, 1, o],
+                parts.at[n, o - 1],
+                sem_g.at[n, 0, 0],
+                sem_g.at[n, 0, 1],
                 member(to),
             ).start()
             return carry
@@ -259,25 +260,16 @@
         lax.fori_loop(1, group, step, 0)
 
     def gram_across(n):
-        def step(o, sums):
-            remote(
-                gsum.at[n, mine],
-                parts.at[n, o],
-                sem_g1.at[n, 0, o],
-                sem_g1.at[n, 1, o],
-                member(ahead(mine, o, group)),
-            ).wait()
-            return sums + parts[n, o]
-
-        sums = lax.fori_loop(1, group, step, gsum[n, mine])
-        zparts[n, 0] = sums
+        others = parts.at[n, 0 : group - 1]
+        wait_all(others, sem_g.at[n, 0, 1])
+        zparts[n, 0] = gsum[n, mine] + jnp.sum(others[...], axis=0)
 
         def send(o, carry):
             remote(
                 zparts.at[n, 0],
                 zparts.at[n, o],
-                sem_g2.at[n, 0, o],
-                sem_g2.at[n, 1, o],
+                sem_g.at[n, 1, 0],
+                sem_g.at[n, 1, 1],
                 at(x, ahead(z, o, nz), c, y),
             ).start()
             return carry
@@ -285,17 +277,7 @@
         lax.fori_loop(1, nz, send, 0)
 
     def gram_gather(n):
-        def step(o, carry):
-            remote(
-                zparts.at[n, 0],
-                zparts.at[n, o],
-                sem_g2.at[n, 0, o],
-                sem_g2.at[n, 1, o],
-                at(x, ahead(z, o, nz), c, y),
-            ).wait()
-            return carry
-
-        lax.fori_loop(1, nz, step, 0)
+        wait_all(zparts.at[n, 1:nz], sem_g.at[n, 1, 1])
 
         def add(plane, sums):
             return sums + zparts[n, lax.rem(z - plane + nz, nz)]
@@ -307,8 +289,8 @@
             remote(
                 gathered.at[n, mine],
                 gathered.at[n, mine],
-                sem_g3.at[n, 0, o],
-                sem_g3.at[n, 1, o],
+                sem_g.at[n, 2, 0],
+                sem_g.at[n, 2, 1],
                 member(ahead(mine, o, group)),
             ).start()
             return carry
@@ -316,18 +298,13 @@
         lax.fori_loop(1, group, send, 0)
 
     def gram_done(n):
-        def step(o, carry):
-            remote(
-                gathered.at[n, mine],
-                gathered.at[n, lax.rem(mine - o + group, group)],
-                sem_g3.at[n, 0, o],
-                sem_g3.at[n, 1, o],
-                member(ahead(mine, o, group)),
-            ).wait()
-            return carry
-
-        lax.fori_loop(1, group, step, 0)
+        wait_all(gathered.at[n, 0 : group - 1], sem_g.at[n, 2, 1])
         return gathered[n].reshape(K, K)
+
+    def gram_sent(n):
+        wait_all(parts.at[n, 0 : group - 1], sem_g.at[n, 0, 0])
+        wait_all(zparts.at[n, 1:nz], sem_g.at[n, 1, 0])
+        wait_all(gathered.at[n, 0 : group - 1], sem_g.at[n, 2, 0])
 
     gsum[0] = lax.dot_general(mine_t, mine_t, NT, preferred_element_type=F32).reshape(
         group, share, K
@@ -358,6 +335,7 @@
             copies_f[o].wait_recv()
         for i in range(nx):
             add_rows(o, i)
+    gram_across(0)
     copies_f[arrivals[-1]].wait_recv()
     copies_c, copies_x = [], []
     for i in range(nx):
@@ -371,7 +349,6 @@
         )
         copy.start()
         copies_c.append(copy)
-    gram_across(0)
     for i in range(nx - 1):
         copies_c[i].wait_recv()
         send_x[i] = (own_c[i, c] + recv_c[i]).astype(BF16)
@@ -385,6 +362,10 @@
         copy.start()
         copies_x.append(copy)
     gram_gather(0)
+
+    identity_beside(work, gram_done(0))
+    factorise(work, PANELS[:-1])
+
     last = nx - 1
     copies_c[last].wait_recv()
     for copy in copies_x:
@@ -409,10 +390,7 @@
             )
             copy.start()
             copies_z.append(copy)
-
-    identity_beside(work, gram_done(0))
-    factorise(work)
-
+    factorise(work, PANELS[-1:])
     block = own_z[...]
     for copy in copies_z:
         copy.wait_recv()
@@ -456,11 +434,10 @@
             at(lax.rem(x + hops + nx, nx), z, c, y),
         )
 
-    def over_c(ox, oz):
-        this = cell(lax.rem(x - ox + nx, nx), lax.rem(z - oz + nz, nz), c)
-        return remote(
-            this, this, sem_lc.at[0, ox, oz], sem_lc.at[1, ox, oz], at(x, z, 1 - c, y)
-        )
+    def over_c(ox):
+        cols = pl.ds(pl.multiple_of(lax.rem(x - ox + nx, nx) * quarter, quarter), quarter)
+        this = loads.at[own_rows, cols]
+        return remote(this, this, sem_lc.at[0, ox], sem_lc.at[1, ox], at(x, z, 1 - c, y))
 
     for o in z_order[:-1]:
         over_z(o).start()
@@ -480,22 +457,24 @@
             start_x(1, oz, 1)
             if nx > 2:
                 start_x(nx - 1, oz, -1)
-            over_c(0, oz).start()
+            if n == nz - 1:
+                over_c(0).start()
         if n >= 2:
             oz = steps[n - 2]
             over_x(1, oz, 1).wait_recv()
             if nx == 4 and n % 2 == 0:
                 start_x(2, oz, 1)
-            over_c(1, oz).start()
             if nx == 4:
                 over_x(3, oz, -1).wait_recv()
                 if n % 2 == 1:
                     start_x(2, oz, -1)
-                over_c(3, oz).start()
+
+    over_c(1).start()
+    if nx == 4:
+        over_c(3).start()
 
     def add_pixels(ox):
-        for oz in steps:
-            over_c(ox, oz).wait_recv()
+        over_c(ox).wait_recv()
         cols = pl.ds(
             pl.multiple_of(lax.rem(x - ox + nx, nx) * quarter, quarter), quarter
         )
@@ -525,7 +504,7 @@
     if nx == 4:
         for n, oz in enumerate(steps):
             over_x(2, oz, 1 if n % 2 == 0 else -1).wait_recv()
-            over_c(2, oz).start()
+        over_c(2).start()
         add_pixels(1)
         add_pixels(3)
     copies_d = add_pixels(nx // 2)
@@ -534,7 +513,7 @@
         copy.wait_recv()
     for o in range(1, ny):
         mine_s = mine_s + (recv_far[...].astype(F32) if 2 * o == ny else recv_d[o - 1])
-    second[y] = mine_s
+    second_out[y] = mine_s
 
     gsum[1] = lax.dot_general(
         mine_s, mine_s, TN, precision=HIGHEST, preferred_element_type=F32
@@ -545,32 +524,36 @@
     copies_s = []
     for o in y_order[:-1]:
         copy = remote(
-            second.at[y],
-            second.at[y],
+            second_out.at[y],
+            second_out.at[y],
             sem_s.at[0, o - 1],
             sem_s.at[1, o - 1],
             at(x, z, c, ahead(y, o, ny)),
         )
         copy.start()
         copies_s.append(copy)
-    identity_beside(work, gram_done(1))
-    factorise(work)
-    factor_out[...] = work[:, :K]
-    for copy in copies_s:
-        copy.wait()
-    for q in range(ny):
-        basis_out[q * ROWS : (q + 1) * ROWS, :] = lax.dot_general(
-            second[q], work[:, K:], NT, precision=HIGHEST, preferred_element_type=F32
-        )
 
     copies = copies_a + list(copies_f.values()) + copies_c + copies_x + copies_z + copies_d
     for copy in copies + copies_lx + [copy_p]:
         copy.wait_send()
-    for oz in range(nz):
-        if oz > 0:
-            over_z(oz).wait_send()
-        for ox in range(nx):
-            over_c(ox, oz).wait_send()
+    for oz in range(1, nz):
+        over_z(oz).wait_send()
+    for ox in range(nx):
+        over_c(ox).wait_send()
+    gram_sent(0)
+
+    identity_beside(work_out, gram_done(1))
+    factorise(work_out, PANELS)
+    gram_sent(1)
+    for copy in copies_s:
+        copy.wait()
+
+
+def basis_kernel(second, work, basis, factor):
+    basis[...] = lax.dot_general(
+        second[0], work[:, K:], NT, precision=HIGHEST, preferred_element_type=F32
+    )
+    factor[...] = work[:, :K]
 
 
 def per_device(dims, data, sketch_matrix):
@@ -582,11 +565,11 @@
     assert rows == ny * ROWS and pixels == nx * quarter
     vm = pltpu.VMEM
     dma = pltpu.SemaphoreType.DMA
-    return pl.pallas_call(
+    second, work = pl.pallas_call(
         functools.partial(sketch_kernel, dims, total),
         out_shape=(
-            jax.ShapeDtypeStruct((rows, K), F32),
-            jax.ShapeDtypeStruct((K, K), F32),
+            jax.ShapeDtypeStruct((ny, ROWS, K), F32),
+            jax.ShapeDtypeStruct((K, 2 * K), F32),
         ),
         in_specs=[pl.BlockSpec(memory_space=pl.ANY)] * 2,
         out_specs=(pl.BlockSpec(memory_space=pltpu.VMEM),) * 2,
@@ -610,7 +593,6 @@
             vm((ny - 1, ROWS, K), F32),
             vm((ROWS, K), BF16),
             vm((ROWS, K), BF16),
-            vm((ny, ROWS, K), F32),
             vm((2, group, share, K), F32),
             vm((2, group, share, K), F32),
             vm((2, group, share, K), F32),
@@ -625,12 +607,10 @@
             dma((2,)),
             dma((2, nz)),
             dma((2, nx, nz)),
-            dma((2, nx, nz)),
+            dma((2, nx)),
             dma((2, ny - 1)),
             dma((2, ny - 1)),
-            dma((2, 2, group)),
-            dma((2, 2, nz)),
-            dma((2, 2, group)),
+            dma((2, 3, 2)),
         ],
         compiler_params=pltpu.CompilerParams(
             collective_id=0, has_side_effects=True, vmem_limit_bytes=60 * 1024 * 1024
@@ -640,6 +620,24 @@
         ),
         name="sketch",
     )(data, sketch_matrix)
+    return pl.pallas_call(
+        basis_kernel,
+        grid=(ny,),
+        out_shape=(
+            jax.ShapeDtypeStruct((rows, K), F32),
+            jax.ShapeDtypeStruct((K, K), F32),
+        ),
+        in_specs=[
+            pl.BlockSpec((1, ROWS, K), lambda q: (q, 0, 0)),
+            pl.BlockSpec((K, 2 * K), lambda q: (0, 0)),
+        ],
+        out_specs=(
+            pl.BlockSpec((ROWS, K), lambda q: (q, 0)),
+            pl.BlockSpec((K, K), lambda q: (0, 0)),
+        ),
+        compiler_params=pltpu.CompilerParams(vmem_limit_bytes=60 * 1024 * 1024),
+        name="basis",
+    )(second, work)
 
 
 def solution(mesh):

time: 146 us -> 148 us (1.014)
  Pallas kernels: 142 us -> 147 us
  local copies, waits for them, and re-layouts: 3.93 us -> 0 us
    pallas_call x0 -> x1, Pallas kernels: none -> 4.37 us  [per_device(): pl.pallas_call(basis_kernel, grid=(ny,), out_shape=(jax.ShapeDtypeStruct(...]
    unnamed x2 -> x0, local copies, waits for them, and re-layouts: 3.93 us -> none
where the time goes in v3:
time: 148 us
  Pallas kernels  147 us (99%)
    pallas_call x1, Pallas kernels, per_device(): pl.pallas_call(functools.partial(sketch_kernel, dims, total), out_shape=(...  143 us
    pallas_call x1, Pallas kernels, per_device(): pl.pallas_call(basis_kernel, grid=(ny,), out_shape=(jax.ShapeDtypeStruct(...  4.37 us

profile of v3, /device:TPU:1, one launch (start us, length us, event | category | flops | bytes accessed | tf_op | source)
XLA Modules:
  0.0 147.8 jit_solution(13834541392273723811)
XLA Ops:
  0.6 142.8 %sketch.1 = (f32[4,256,256]{2,1,0:T(8,128)}, f32[256,512]{1,0:T(8,128)}) custom-call(bf16[1024,4096]{1,0:T(8,128)(2,1)} %data_hbm.1, bf16[4096,256]{1,0:T(8,128)(2,1)} %sketch_hbm.1), custom_call_target="tpu_custom_call" | custom-call | flops 6442450944 | bytes 8388608 | tf_op jit(solution)/shard_map/sketch/pallas_call | solution.py:568
  143.4 4.4 %basis.1 = (f32[1024,256]{1,0:T(8,128)}, f32[256,256]{1,0:T(8,128)}) custom-call(f32[4,256,256]{2,1,0:T(8,128)} %get-tuple-element.4.second, f32[256,512]{1,0:T(8,128)} %get-tuple-element.5.work), custom_call_target="tpu_custom_call" | custom-call | tf_op jit(solution)/shard_map/basis/pallas_call | solution.py:623

commit v4 on v3

--- a/solution.py
+++ b/solution.py
@@ -311,17 +311,20 @@
     )
     gram_scatter(0)
 
-    def add_rows(o, i):
-        block_at = lax.rem(y - o + ny, ny)
+    def add_rows(offsets, i):
         xd = ahead(x, x_order[i], nx)
 
         def tile(t, carry):
             cols = pl.ds(pl.multiple_of(xd * quarter + t * ROWS, ROWS), ROWS)
             here = pl.ds(pl.multiple_of(t * ROWS, ROWS), ROWS)
-            block = jnp.dot(
-                first_t[block_at], data[rows_of(block_at), cols], preferred_element_type=F32
-            ).reshape(nc, half, ROWS)
-            if o == 0:
+            block = jnp.zeros((K, ROWS), F32)
+            for o in offsets:
+                block_at = lax.rem(y - o + ny, ny)
+                block += jnp.dot(
+                    first_t[block_at], data[rows_of(block_at), cols], preferred_element_type=F32
+                )
+            block = block.reshape(nc, half, ROWS)
+            if 0 in offsets:
                 own_c[i, :, :, here] = block
             else:
                 own_c[i, :, :, here] += block
@@ -329,17 +332,14 @@
 
         lax.fori_loop(0, quarter // ROWS, tile, 0)
 
-    arrivals = y_order[::-1]
-    for o in arrivals[:-1]:
-        if o > 0:
-            copies_f[o].wait_recv()
-        for i in range(nx):
-            add_rows(o, i)
+    for i in range(nx):
+        add_rows([0], i)
+    for copy in copies_f.values():
+        copy.wait_recv()
     gram_across(0)
-    copies_f[arrivals[-1]].wait_recv()
     copies_c, copies_x = [], []
     for i in range(nx):
-        add_rows(arrivals[-1], i)
+        add_rows(range(1, ny), i)
         copy = remote(
             own_c.at[i, 1 - c],
             recv_c.at[i],
@@ -349,22 +349,23 @@
         )
         copy.start()
         copies_c.append(copy)
-    for i in range(nx - 1):
-        copies_c[i].wait_recv()
-        send_x[i] = (own_c[i, c] + recv_c[i]).astype(BF16)
-        copy = remote(
-            send_x.at[i],
-            recv_x.at[i],
-            sem_x.at[0, i],
-            sem_x.at[1, i],
-            at(ahead(x, x_order[i], nx), z, c, y),
-        )
-        copy.start()
-        copies_x.append(copy)
+        if i > 0:
+            j = i - 1
+            copies_c[j].wait_recv()
+            send_x[j] = (own_c[j, c] + recv_c[j]).astype(BF16)
+            copy = remote(
+                send_x.at[j],
+                recv_x.at[j],
+                sem_x.at[0, j],
+                sem_x.at[1, j],
+                at(ahead(x, x_order[j], nx), z, c, y),
+            )
+            copy.start()
+            copies_x.append(copy)
     gram_gather(0)
 
     identity_beside(work, gram_done(0))
-    factorise(work, PANELS[:-1])
+    factorise(work, PANELS[:2])
 
     last = nx - 1
     copies_c[last].wait_recv()
@@ -390,7 +391,7 @@
             )
             copy.start()
             copies_z.append(copy)
-    factorise(work, PANELS[-1:])
+    factorise(work, PANELS[2:])
     block = own_z[...]
     for copy in copies_z:
         copy.wait_recv()

time: 148 us -> 141 us (0.953)
  Pallas kernels: 147 us -> 140 us
    pallas_call x1, Pallas kernels: 143 us -> 136 us  [per_device(): pl.pallas_call(functools.partial(sketch_kernel, dims, total), out_shape=(...]
where the time goes in v4:
time: 141 us
  Pallas kernels  140 us (99%)
    pallas_call x1, Pallas kernels, per_device(): pl.pallas_call(functools.partial(sketch_kernel, dims, total), out_shape=(...  136 us
    pallas_call x1, Pallas kernels, per_device(): pl.pallas_call(basis_kernel, grid=(ny,), out_shape=(jax.ShapeDtypeStruct(...  4.36 us

profile of v4, /device:TPU:1, one launch (start us, length us, event | category | flops | bytes accessed | tf_op | source)
XLA Modules:
  0.0 140.5 jit_solution(16989765511162714571)
XLA Ops:
  0.6 135.5 %sketch.1 = (f32[4,256,256]{2,1,0:T(8,128)}, f32[256,512]{1,0:T(8,128)}) custom-call(bf16[1024,4096]{1,0:T(8,128)(2,1)} %data_hbm.1, bf16[4096,256]{1,0:T(8,128)(2,1)} %sketch_hbm.1), custom_call_target="tpu_custom_call" | custom-call | flops 6442450944 | bytes 8388608 | tf_op jit(solution)/shard_map/sketch/pallas_call | solution.py:569
  136.2 4.4 %basis.1 = (f32[1024,256]{1,0:T(8,128)}, f32[256,256]{1,0:T(8,128)}) custom-call(f32[4,256,256]{2,1,0:T(8,128)} %get-tuple-element.4.second, f32[256,512]{1,0:T(8,128)} %get-tuple-element.5.work), custom_call_target="tpu_custom_call" | custom-call | tf_op jit(solution)/shard_map/basis/pallas_call | solution.py:624

commit v5 on v4

--- a/solution.py
+++ b/solution.py
@@ -18,6 +18,7 @@
 PANELS = range(K // PANEL)
 SUB = 8
 
+NN = (((1,), (0,)), ((), ()))
 NT = (((1,), (1,)), ((), ()))
 TN = (((0,), (0,)), ((), ()))
 
@@ -57,9 +58,11 @@
             pivots = jnp.where(sub == j, pivot, pivots)
             heads = [panel[k][j : j + 1, :] for k in range(SUB)]
             row = top[j : j + 1, :]
-            below = jnp.where(sub > j, panel[j], 0.0) * inverse
+            under = jnp.where(sub > j, panel[j], 0.0)
+            below = under * inverse
             for k in range(j + 1, SUB):
-                panel[k] = panel[k] - below * heads[k]
+                term = (under * heads[k]) * inverse if k == j + 1 else below * heads[k]
+                panel[k] = panel[k] - term
             top = top - below * row
             for h in range(g + 1, groups):
                 scaled = cols[h][j] * inverse
@@ -69,6 +72,20 @@
         done.append(jnp.where(lane >= sub + at, top * lax.rsqrt(pivots), 0.0))
     state = jnp.concatenate(done, axis=0)
     return state[:, :n], state[:, n:]
+
+
+def split(value):
+    high = value.astype(BF16)
+    return high, (value - high.astype(F32)).astype(BF16)
+
+
+def dot_split(a, b, numbers):
+    a_high, a_low = split(a)
+    b_high, b_low = split(b)
+    dot = functools.partial(
+        lax.dot_general, dimension_numbers=numbers, preferred_element_type=F32
+    )
+    return dot(a_high, b_high) + (dot(a_high, b_low) + dot(a_low, b_high))
 
 
 def factorise(work, panels, size=K):
@@ -198,8 +215,8 @@
         )
         return carry
 
-    lax.fori_loop(1, group, greet_group, 0)
-    lax.fori_loop(1, nz, greet_z, 0)
+    lax.fori_loop(1, group, greet_group, 0, unroll=True)
+    lax.fori_loop(1, nz, greet_z, 0, unroll=True)
     sketch_load.wait()
 
     copies_a = []
@@ -257,7 +274,7 @@
             ).start()
             return carry
 
-        lax.fori_loop(1, group, step, 0)
+        lax.fori_loop(1, group, step, 0, unroll=True)
 
     def gram_across(n):
         others = parts.at[n, 0 : group - 1]
@@ -274,7 +291,7 @@
             ).start()
             return carry
 
-        lax.fori_loop(1, nz, send, 0)
+        lax.fori_loop(1, nz, send, 0, unroll=True)
 
     def gram_gather(n):
         wait_all(zparts.at[n, 1:nz], sem_g.at[n, 1, 1])
@@ -282,7 +299,7 @@
         def add(plane, sums):
             return sums + zparts[n, lax.rem(z - plane + nz, nz)]
 
-        sums = lax.fori_loop(0, nz, add, jnp.zeros((share, K), F32))
+        sums = lax.fori_loop(0, nz, add, jnp.zeros((share, K), F32), unroll=True)
         gathered[n, mine] = sums * (1.0 / total)
 
         def send(o, carry):
@@ -295,7 +312,7 @@
             ).start()
             return carry
 
-        lax.fori_loop(1, group, send, 0)
+        lax.fori_loop(1, group, send, 0, unroll=True)
 
     def gram_done(n):
         wait_all(gathered.at[n, 0 : group - 1], sem_g.at[n, 2, 1])
@@ -349,23 +366,22 @@
         )
         copy.start()
         copies_c.append(copy)
-        if i > 0:
-            j = i - 1
-            copies_c[j].wait_recv()
-            send_x[j] = (own_c[j, c] + recv_c[j]).astype(BF16)
-            copy = remote(
-                send_x.at[j],
-                recv_x.at[j],
-                sem_x.at[0, j],
-                sem_x.at[1, j],
-                at(ahead(x, x_order[j], nx), z, c, y),
-            )
-            copy.start()
-            copies_x.append(copy)
     gram_gather(0)
+    for i in range(nx - 1):
+        copies_c[i].wait_recv()
+        send_x[i] = (own_c[i, c] + recv_c[i]).astype(BF16)
+        copy = remote(
+            send_x.at[i],
+            recv_x.at[i],
+            sem_x.at[0, i],
+            sem_x.at[1, i],
+            at(ahead(x, x_order[i], nx), z, c, y),
+        )
+        copy.start()
+        copies_x.append(copy)
 
     identity_beside(work, gram_done(0))
-    factorise(work, PANELS[:2])
+    factorise(work, PANELS[:3])
 
     last = nx - 1
     copies_c[last].wait_recv()
@@ -391,7 +407,7 @@
             )
             copy.start()
             copies_z.append(copy)
-    factorise(work, PANELS[2:])
+    factorise(work, PANELS[3:])
     block = own_z[...]
     for copy in copies_z:
         copy.wait_recv()
@@ -403,12 +419,7 @@
     copy_p.wait_recv()
 
     own_rows = pl.ds(pl.multiple_of(c * half, half), half)
-    solved = jnp.dot(
-        work[own_rows, K:],
-        pair[...].reshape(K, LANES),
-        precision=HIGHEST,
-        preferred_element_type=F32,
-    )
+    solved = dot_split(work[own_rows, K:], pair[...].reshape(K, LANES), NN)
 
     def cell(px, pz, pc):
         cols = pl.ds(pl.multiple_of((px * nz + pz) * LANES, LANES), LANES)
@@ -551,9 +562,8 @@
 
 
 def basis_kernel(second, work, basis, factor):
-    basis[...] = lax.dot_general(
-        second[0], work[:, K:], NT, precision=HIGHEST, preferred_element_type=F32
-    )
+    for q in range(second.shape[0]):
+        basis[q * ROWS : (q + 1) * ROWS, :] = dot_split(second[q], work[:, K:], NT)
     factor[...] = work[:, :K]
 
 
@@ -623,17 +633,17 @@
     )(data, sketch_matrix)
     return pl.pallas_call(
         basis_kernel,
-        grid=(ny,),
+        grid=(2,),
         out_shape=(
             jax.ShapeDtypeStruct((rows, K), F32),
             jax.ShapeDtypeStruct((K, K), F32),
         ),
         in_specs=[
-            pl.BlockSpec((1, ROWS, K), lambda q: (q, 0, 0)),
+            pl.BlockSpec((ny // 2, ROWS, K), lambda q: (q, 0, 0)),
             pl.BlockSpec((K, 2 * K), lambda q: (0, 0)),
         ],
         out_specs=(
-            pl.BlockSpec((ROWS, K), lambda q: (q, 0)),
+            pl.BlockSpec((rows // 2, K), lambda q: (q, 0)),
             pl.BlockSpec((K, K), lambda q: (0, 0)),
         ),
         compiler_params=pltpu.CompilerParams(vmem_limit_bytes=60 * 1024 * 1024),

time: 141 us -> 136 us (0.965)
  Pallas kernels: 140 us -> 135 us
    pallas_call x1, Pallas kernels: 136 us -> 132 us  [per_device(): pl.pallas_call(functools.partial(sketch_kernel, dims, total), out_shape=(...]
    pallas_call x1, Pallas kernels: 4.36 us -> 2.85 us  [per_device(): pl.pallas_call(basis_kernel, grid=(2,), out_shape=(jax.ShapeDtypeStruct((...]
where the time goes in v5:
time: 136 us
  Pallas kernels  135 us (99%)
    pallas_call x1, Pallas kernels, per_device(): pl.pallas_call(functools.partial(sketch_kernel, dims, total), out_shape=(...  132 us
    pallas_call x1, Pallas kernels, per_device(): pl.pallas_call(basis_kernel, grid=(2,), out_shape=(jax.ShapeDtypeStruct((...  2.85 us

profile of v5, /device:TPU:1, one launch (start us, length us, event | category | flops | bytes accessed | tf_op | source)
XLA Modules:
  0.0 136.0 jit_solution(11930480454397553642)
XLA Ops:
  0.6 132.5 %sketch.1 = (f32[4,256,256]{2,1,0:T(8,128)}, f32[256,512]{1,0:T(8,128)}) custom-call(bf16[1024,4096]{1,0:T(8,128)(2,1)} %data_hbm.1, bf16[4096,256]{1,0:T(8,128)(2,1)} %sketch_hbm.1), custom_call_target="tpu_custom_call" | custom-call | flops 6442450944 | bytes 8388608 | tf_op jit(solution)/shard_map/sketch/pallas_call | solution.py:579
  133.1 2.9 %basis.1 = (f32[1024,256]{1,0:T(8,128)}, f32[256,256]{1,0:T(8,128)}) custom-call(f32[4,256,256]{2,1,0:T(8,128)} %get-tuple-element.4.second, f32[256,512]{1,0:T(8,128)} %get-tuple-element.5.work), custom_call_target="tpu_custom_call" | custom-call | tf_op jit(solution)/shard_map/basis/pallas_call | solution.py:634

commit v6 on v5

--- a/solution.py
+++ b/solution.py
@@ -89,18 +89,36 @@
 
 
 def factorise(work, panels, size=K):
+    square = None
     for b in panels:
         lo, hi = b * PANEL, (b + 1) * PANEL
-        upper, inverse = factor_panel(work[lo:hi, lo:hi])
-        top = jnp.dot(inverse, work[lo:hi, :], precision=HIGHEST, preferred_element_type=F32)
+        if square is None:
+            square = work[lo:hi, lo:hi]
+        upper, inverse = factor_panel(square)
+        left, right = lo // LANES * LANES, size + -(-hi // LANES) * LANES
+        top = jnp.dot(
+            inverse, work[lo:hi, left:right], precision=HIGHEST, preferred_element_type=F32
+        )
         at_row = lax.broadcasted_iota(jnp.int32, top.shape, 0) + lo
-        at_col = lax.broadcasted_iota(jnp.int32, top.shape, 1)
+        at_col = lax.broadcasted_iota(jnp.int32, top.shape, 1) + left
         top = jnp.where(at_col >= at_row, top, 0.0)
-        work[lo:hi, :] = top
         if hi < size:
-            work[hi:, :] -= lax.dot_general(
-                top[:, hi:size], top, TN, precision=HIGHEST, preferred_element_type=F32
+            ahead = top[:, hi - left : hi + PANEL - left]
+            square = work[hi : hi + PANEL, hi : hi + PANEL] - lax.dot_general(
+                ahead, ahead, TN, precision=HIGHEST, preferred_element_type=F32
             )
+            work[hi:, left:right] -= lax.dot_general(
+                top[:, hi - left : size - left],
+                top,
+                TN,
+                precision=HIGHEST,
+                preferred_element_type=F32,
+            )
+        if left > 0:
+            work[lo:hi, :left] = jnp.zeros((PANEL, left), F32)
+        work[lo:hi, left:right] = top
+        if right < 2 * size:
+            work[lo:hi, right:] = jnp.zeros((PANEL, 2 * size - right), F32)
 
 
 def identity_beside(work, gram, size=K):
@@ -461,6 +479,7 @@
         copy.start()
         copies_lx.append(copy)
 
+    relayed = nz - 3
     for n in range(nz + 2):
         if n < nz:
             oz = steps[n]
@@ -469,16 +488,18 @@
             start_x(1, oz, 1)
             if nx > 2:
                 start_x(nx - 1, oz, -1)
+            if nx == 4 and n >= relayed:
+                start_x(2, oz, 2)
             if n == nz - 1:
                 over_c(0).start()
         if n >= 2:
             oz = steps[n - 2]
             over_x(1, oz, 1).wait_recv()
-            if nx == 4 and n % 2 == 0:
+            if nx == 4 and n - 2 < relayed and n % 2 == 0:
                 start_x(2, oz, 1)
             if nx == 4:
                 over_x(3, oz, -1).wait_recv()
-                if n % 2 == 1:
+                if n - 2 < relayed and n % 2 == 1:
                     start_x(2, oz, -1)
 
     over_c(1).start()

time: 136 us -> 134 us (0.985)
  Pallas kernels: 135 us -> 133 us
    pallas_call x1, Pallas kernels: 132 us -> 130 us  [per_device(): pl.pallas_call(functools.partial(sketch_kernel, dims, total), out_shape=(...]
where the time goes in v6:
time: 134 us
  Pallas kernels  133 us (99%)
    pallas_call x1, Pallas kernels, per_device(): pl.pallas_call(functools.partial(sketch_kernel, dims, total), out_shape=(...  130 us
    pallas_call x1, Pallas kernels, per_device(): pl.pallas_call(basis_kernel, grid=(2,), out_shape=(jax.ShapeDtypeStruct((...  2.85 us

profile of v6, /device:TPU:1, one launch (start us, length us, event | category | flops | bytes accessed | tf_op | source)
XLA Modules:
  0.0 134.0 jit_solution(15180864789571773906)
XLA Ops:
  0.6 130.5 %sketch.1 = (f32[4,256,256]{2,1,0:T(8,128)}, f32[256,512]{1,0:T(8,128)}) custom-call(bf16[1024,4096]{1,0:T(8,128)(2,1)} %data_hbm.1, bf16[4096,256]{1,0:T(8,128)(2,1)} %sketch_hbm.1), custom_call_target="tpu_custom_call" | custom-call | flops 6442450944 | bytes 8388608 | tf_op jit(solution)/shard_map/sketch/pallas_call | solution.py:600
  131.1 2.9 %basis.1 = (f32[1024,256]{1,0:T(8,128)}, f32[256,256]{1,0:T(8,128)}) custom-call(f32[4,256,256]{2,1,0:T(8,128)} %get-tuple-element.4.second, f32[256,512]{1,0:T(8,128)} %get-tuple-element.5.work), custom_call_target="tpu_custom_call" | custom-call | tf_op jit(solution)/shard_map/basis/pallas_call | solution.py:655

commit v7 on v6

--- a/solution.py
+++ b/solution.py
@@ -399,7 +399,7 @@
         copies_x.append(copy)
 
     identity_beside(work, gram_done(0))
-    factorise(work, PANELS[:3])
+    factorise(work, PANELS[:2])
 
     last = nx - 1
     copies_c[last].wait_recv()
@@ -425,7 +425,7 @@
             )
             copy.start()
             copies_z.append(copy)
-    factorise(work, PANELS[3:])
+    factorise(work, PANELS[2:])
     block = own_z[...]
     for copy in copies_z:
         copy.wait_recv()

time: 134 us -> 133 us (level)
    pallas_call x1, Pallas kernels: 130 us -> 129 us  [per_device(): pl.pallas_call(functools.partial(sketch_kernel, dims, total), out_shape=(...]
where the time goes in v7:
time: 133 us; the launch traced here: 132 us
  Pallas kernels  132 us (99%)
    pallas_call x1, Pallas kernels, per_device(): pl.pallas_call(functools.partial(sketch_kernel, dims, total), out_shape=(...  129 us
    pallas_call x1, Pallas kernels, per_device(): pl.pallas_call(basis_kernel, grid=(2,), out_shape=(jax.ShapeDtypeStruct((...  2.85 us

profile of v7, /device:TPU:1, one launch (start us, length us, event | category | flops | bytes accessed | tf_op | source)
XLA Modules:
  0.0 132.5 jit_solution(13354323156124551598)
XLA Ops:
  0.6 129.0 %sketch.1 = (f32[4,256,256]{2,1,0:T(8,128)}, f32[256,512]{1,0:T(8,128)}) custom-call(bf16[1024,4096]{1,0:T(8,128)(2,1)} %data_hbm.1, bf16[4096,256]{1,0:T(8,128)(2,1)} %sketch_hbm.1), custom_call_target="tpu_custom_call" | custom-call | flops 6442450944 | bytes 8388608 | tf_op jit(solution)/shard_map/sketch/pallas_call | solution.py:600
  129.6 2.9 %basis.1 = (f32[1024,256]{1,0:T(8,128)}, f32[256,256]{1,0:T(8,128)}) custom-call(f32[4,256,256]{2,1,0:T(8,128)} %get-tuple-element.4.second, f32[256,512]{1,0:T(8,128)} %get-tuple-element.5.work), custom_call_target="tpu_custom_call" | custom-call | tf_op jit(solution)/shard_map/basis/pallas_call | solution.py:655

commit v8 on v7

--- a/solution.py
+++ b/solution.py
@@ -399,7 +399,7 @@
         copies_x.append(copy)
 
     identity_beside(work, gram_done(0))
-    factorise(work, PANELS[:2])
+    factorise(work, PANELS[:1])
 
     last = nx - 1
     copies_c[last].wait_recv()
@@ -425,7 +425,7 @@
             )
             copy.start()
             copies_z.append(copy)
-    factorise(work, PANELS[2:])
+    factorise(work, PANELS[1:])
     block = own_z[...]
     for copy in copies_z:
         copy.wait_recv()

time: 133 us -> 132 us (level)
  no operation moved by 1% of the time
where the time goes in v8:
time: 132 us
  Pallas kernels  131 us (99%)
    pallas_call x1, Pallas kernels, per_device(): pl.pallas_call(functools.partial(sketch_kernel, dims, total), out_shape=(...  128 us
    pallas_call x1, Pallas kernels, per_device(): pl.pallas_call(basis_kernel, grid=(2,), out_shape=(jax.ShapeDtypeStruct((...  2.85 us

profile of v8, /device:TPU:1, one launch (start us, length us, event | category | flops | bytes accessed | tf_op | source)
XLA Modules:
  0.0 132.0 jit_solution(6676325725950716228)
XLA Ops:
  0.6 128.5 %sketch.1 = (f32[4,256,256]{2,1,0:T(8,128)}, f32[256,512]{1,0:T(8,128)}) custom-call(bf16[1024,4096]{1,0:T(8,128)(2,1)} %data_hbm.1, bf16[4096,256]{1,0:T(8,128)(2,1)} %sketch_hbm.1), custom_call_target="tpu_custom_call" | custom-call | flops 6442450944 | bytes 8388608 | tf_op jit(solution)/shard_map/sketch/pallas_call | solution.py:600
  129.1 2.9 %basis.1 = (f32[1024,256]{1,0:T(8,128)}, f32[256,256]{1,0:T(8,128)}) custom-call(f32[4,256,256]{2,1,0:T(8,128)} %get-tuple-element.4.second, f32[256,512]{1,0:T(8,128)} %get-tuple-element.5.work), custom_call_target="tpu_custom_call" | custom-call | tf_op jit(solution)/shard_map/basis/pallas_call | solution.py:655

commit v9 on v8

--- a/solution.py
+++ b/solution.py
@@ -373,6 +373,20 @@
         copy.wait_recv()
     gram_across(0)
     copies_c, copies_x = [], []
+
+    def send_over_x(i):
+        copies_c[i].wait_recv()
+        send_x[i] = (own_c[i, c] + recv_c[i]).astype(BF16)
+        copy = remote(
+            send_x.at[i],
+            recv_x.at[i],
+            sem_x.at[0, i],
+            sem_x.at[1, i],
+            at(ahead(x, x_order[i], nx), z, c, y),
+        )
+        copy.start()
+        copies_x.append(copy)
+
     for i in range(nx):
         add_rows(range(1, ny), i)
         copy = remote(
@@ -384,19 +398,11 @@
         )
         copy.start()
         copies_c.append(copy)
+        if i == 1:
+            send_over_x(0)
     gram_gather(0)
-    for i in range(nx - 1):
-        copies_c[i].wait_recv()
-        send_x[i] = (own_c[i, c] + recv_c[i]).astype(BF16)
-        copy = remote(
-            send_x.at[i],
-            recv_x.at[i],
-            sem_x.at[0, i],
-            sem_x.at[1, i],
-            at(ahead(x, x_order[i], nx), z, c, y),
-        )
-        copy.start()
-        copies_x.append(copy)
+    for i in range(1, nx - 1):
+        send_over_x(i)
 
     identity_beside(work, gram_done(0))
     factorise(work, PANELS[:1])

time: 132 us -> 130 us (0.985)
    pallas_call x1, Pallas kernels: 128 us -> 127 us  [per_device(): pl.pallas_call(functools.partial(sketch_kernel, dims, total), out_shape=(...]
where the time goes in v9:
time: 130 us
  Pallas kernels  130 us (100%)
    pallas_call x1, Pallas kernels, per_device(): pl.pallas_call(functools.partial(sketch_kernel, dims, total), out_shape=(...  127 us
    pallas_call x1, Pallas kernels, per_device(): pl.pallas_call(basis_kernel, grid=(2,), out_shape=(jax.ShapeDtypeStruct((...  2.85 us

profile of v9, /device:TPU:1, one launch (start us, length us, event | category | flops | bytes accessed | tf_op | source)
XLA Modules:
  0.0 130.3 jit_solution(1218003588678505476)
XLA Ops:
  0.6 126.8 %sketch.1 = (f32[4,256,256]{2,1,0:T(8,128)}, f32[256,512]{1,0:T(8,128)}) custom-call(bf16[1024,4096]{1,0:T(8,128)(2,1)} %data_hbm.1, bf16[4096,256]{1,0:T(8,128)(2,1)} %sketch_hbm.1), custom_call_target="tpu_custom_call" | custom-call | flops 6442450944 | bytes 8388608 | tf_op jit(solution)/shard_map/sketch/pallas_call | solution.py:606
  127.5 2.9 %basis.1 = (f32[1024,256]{1,0:T(8,128)}, f32[256,256]{1,0:T(8,128)}) custom-call(f32[4,256,256]{2,1,0:T(8,128)} %get-tuple-element.4.second, f32[256,512]{1,0:T(8,128)} %get-tuple-element.5.work), custom_call_target="tpu_custom_call" | custom-call | tf_op jit(solution)/shard_map/basis/pallas_call | solution.py:661
